TPU v7x, 32 devices: a whole 2x2x4 slice. The times are simulated.
32 devices in a mesh: var: 16 (over z, x, core), samp: 2 (over y).
Axes of the slice: x: 2, y: 2, z: 4, core: 2. Of those that a mesh axis runs over, the one named last changes fastest.
Arguments:
- observed: bfloat16 [1024, 16384], P('samp', 'var'), may hold values from -40 to 40
- pattern: int32 [128, 3], P('var'), may hold values from 0 to 127, as said below
- omega_init: bfloat16 [128, 3, 128, 128], P('var'), may hold values from -4 to 4
Outputs:
- precision: float32 [128, 3, 128, 128], P(('var', 'samp'))
Inputs may be any that keep to these rules, and one draw needn't show every extreme that they name: pattern[R, 0] = R. The other two blocks of row block R belong to two different var devices among the four whose index differs from the owner of R by 1 or 2 (counted modulo the number of var devices). On every var device each of those four devices supplies the second block of exactly two of its row blocks.
All inputs are finite; a program needn't handle non-finite values.
Results may differ from a plain program's by a relative error of at most 0.0044.
Values may be sent and summed in bfloat16 or wider, within the bound.
A program may use at most 64 MiB of HBM per device.

v0:
```python
import jax
import jax.numpy as jnp
from jax import lax
from jax.sharding import PartitionSpec as P

ITERS = 2


STEP_SCALE = 0.5
THRESHOLD = 0.25
EPSILON = 1e-06


def from_behind(block, axis, distance):
    devices = range(lax.axis_size(axis))
    route = [((i - distance) % len(devices), i) for i in devices]
    return lax.ppermute(block, axis, route)


def proximal(iterate, grad, mean_sq, diag_mask):
    step_size = STEP_SCALE / jnp.sqrt(mean_sq + EPSILON)
    stepped = iterate - step_size * grad
    shrunk = stepped - jnp.clip(stepped, -THRESHOLD, THRESHOLD)
    barrier = 0.5 * (stepped + jnp.sqrt(stepped * stepped + 4.0 * step_size))
    return jnp.where(diag_mask, barrier, shrunk)


def block_terms(packed, selected, inverse):
    weighted = jnp.einsum("rkab,nrkb->rna", packed, selected, preferred_element_type=jnp.float32)
    weighted = weighted.astype(jnp.bfloat16)
    return (
        jnp.einsum("rna,nrkb->rkab", weighted, selected, preferred_element_type=jnp.float32)
        * inverse
    )


def body(observed, pattern, omega_init):
    var_count = lax.axis_size("var")
    samp_count = lax.axis_size("samp")
    var_index = lax.axis_index("var")
    samp_index = lax.axis_index("samp")
    row_blocks = omega_init.shape[0]
    slot_count = omega_init.shape[1]
    block_size = omega_init.shape[2]
    sample_rows = observed.shape[0]
    inverse = 1.0 / (sample_rows * samp_count)
    below_one = from_behind(observed, "var", 1)
    above_one = from_behind(observed, "var", -1)
    below_two = from_behind(observed, "var", 2)
    above_two = from_behind(observed, "var", -2)
    strips = jnp.concatenate((below_two, below_one, observed, above_one, above_two), axis=1)
    blocks = strips.reshape(sample_rows, 5 * row_blocks, block_size)
    owners = pattern // row_blocks
    within = pattern % row_blocks
    offsets = (owners - var_index + var_count + 2) % var_count
    slot_index = (offsets * row_blocks + within).reshape(-1)
    selected = jnp.take(blocks, slot_index, axis=1).reshape(
        sample_rows, row_blocks, slot_count, block_size
    )
    slot_ids = lax.broadcasted_iota(jnp.int32, (slot_count, block_size, block_size), 0)
    row_ids = lax.broadcasted_iota(jnp.int32, (slot_count, block_size, block_size), 1)
    col_ids = lax.broadcasted_iota(jnp.int32, (slot_count, block_size, block_size), 2)
    diag_mask = (slot_ids == 0) & (row_ids == col_ids)
    entries = row_blocks * slot_count * block_size * block_size * var_count
    share_rows = row_blocks // samp_count
    iterate = omega_init.astype(jnp.float32)
    for iteration in range(ITERS):
        packed = iterate.astype(jnp.bfloat16)
        partial_grad = block_terms(packed, selected, inverse)
        grad = lax.psum(partial_grad, "samp")
        squares = lax.psum(jnp.sum(grad * grad), "var")
        iterate = proximal(iterate, grad, squares / entries, diag_mask)
    return lax.dynamic_slice_in_dim(iterate, samp_index * share_rows, share_rows, 0)


def solution(mesh):
    return jax.shard_map(
        body,
        mesh=mesh,
        in_specs=(P("samp", "var"), P("var", None), P("var", None, None, None)),
        out_specs=P(("var", "samp"), None, None, None),
        check_vma=False,
    )
```

profile of v0, /device:TPU:0, one launch (start us, length us, event | category | flops | bytes accessed | tf_op | source)
XLA Modules:
  0.0 298.1 jit_solution(18140700859700650600)
XLA Ops:
  6.5 1.5 copy.16
  8.1 3.0 %collective-permute-start = (bf16[512,1024]{0,1:T(8,128)(2,1)S(1)}, bf16[512,1024]{0,1:T(8,128)(2,1)}, u32[]{:S(2)}, u32[]{:S(2)}) collective-permute-start(bf16[512,1024]{0,1:T(8,128)(2,1)S(1)} %copy.16), channel_id=1, source_target_pairs={{28,0},{30,2},{0,4},{2,6},{4,8},{6,10},{8,12},{10,14},{12,16},{14,... | collective-permute-start | bytes 3145736 | tf_op jit(solution)/shard_map/ppermute | solution.py:17
  11.0 4.4 %collective-permute-start.2 = (bf16[512,1024]{0,1:T(8,128)(2,1)S(1)}, bf16[512,1024]{0,1:T(8,128)(2,1)S(1)}, u32[]{:S(2)}, u32[]{:S(2)}) collective-permute-start(bf16[512,1024]{0,1:T(8,128)(2,1)S(1)} %copy.16), channel_id=1, source_target_pairs={{2,0},{4,2},{6,4},{8,6},{10,8},{12,10},{14,12},{16,14},{18,16},{20... | collective-permute-start | bytes 3145736 | tf_op jit(solution)/shard_map/ppermute | solution.py:17
  15.5 0.4 collective-permute-start.3
  16.2 52.1 %collective-permute-done = bf16[512,1024]{0,1:T(8,128)(2,1)} collective-permute-done((bf16[512,1024]{0,1:T(8,128)(2,1)S(1)}, bf16[512,1024]{0,1:T(8,128)(2,1)}, u32[]{:S(2)}, u32[]{:S(2)}) %collective-permute-start) | collective-permute-done | bytes 1048608 | tf_op jit(solution)/shard_map/ppermute | solution.py:17
  68.3 2.3 constant_dynamic-update-slice_fusion.4
  70.6 2.3 constant_dynamic-update-slice_fusion.3
  72.9 1.1 constant_dynamic-update-slice_fusion.2
  74.0 1.1 constant_dynamic-update-slice_fusion.1
  75.0 7.2 %collective-permute-done.3 = bf16[512,1024]{0,1:T(8,128)(2,1)S(1)} collective-permute-done((bf16[512,1024]{0,1:T(8,128)(2,1)S(1)}, bf16[512,1024]{0,1:T(8,128)(2,1)S(1)}, u32[]{:S(2)}, u32[]{:S(2)}) %collective-permute-start.3) | collective-permute-done | bytes 1048608 | tf_op jit(solution)/shard_map/ppermute | solution.py:17
  82.2 1.0 constant_dynamic-update-slice_fusion
  83.2 7.9 %copy.22 = bf16[512,40,128]{2,0,1:T(8,128)(2,1)} copy(bf16[512,40,128]{0,2,1:T(8,128)(2,1)} %bitcast) | data formatting | bytes 10485760 | tf_op jit(solution)/shard_map/reshape | solution.py:52
  91.1 3.6 %gather_fusion = bf16[24,512,128]{2,1,0:T(8,128)(2,1)S(1)} fusion(bf16[512,40,128]{2,0,1:T(8,128)(2,1)} %copy.22, s32[1024]{0:T(1024)S(1)} %pad_clamp_fusion), kind=kCustom, calls=%fused_computation | custom fusion | bytes 6291552 | tf_op jit(solution)/shard_map/jit(_take)/gather | solution.py:57
  94.8 2.8 copy.23
  97.6 6.2 %multiply_bitcast_fusion.1 = f32[8,3,128,128]{2,3,1,0:T(8,128)} fusion(bf16[512,8,3,128]{0,3,2,1:T(8,128)(2,1)} %copy.23, pred[8,3]{1,0:T(8,128)(4,1)S(1)} %copy.15, bf16[8,3,128,128]{3,2,1,0:T(8,128)(2,1)} %param.5), kind=kOutput, calls=%fused_computation.14 | convolution fusion | flops 809369600 | bytes 5505048 | tf_op jit(solution)/shard_map/rna,nrkb->rkab/dot_general | solution.py:32
  104.0 54.5 %all-reduce.3.cloned.1.call-done = f32[8,3,128,128]{2,3,1,0:T(8,128)} async-done(((f32[8,3,128,128]{2,3,1,0:T(8,128)}), f32[8,3,128,128]{2,3,1,0:T(8,128)}) %all-reduce.3.cloned.1.call-update) | async-done | bytes 1572880 | tf_op jit(solution)/shard_map/psum | solution.py:70
  158.5 2.5 multiply_reduce_fusion.1
  161.4 33.8 %psum.29 = f32[]{:T(128)} all-reduce(f32[]{:T(128)} %multiply_reduce_fusion.1), channel_id=1, replica_groups=mesh['var'=16,'samp'=2] {'var'}, use_global_device_ids=true, to_apply=%region_2.3 | all-reduce | flops 1 | bytes 8 | tf_op jit(solution)/shard_map/psum | solution.py:71
  195.8 6.9 %multiply_bitcast_fusion = f32[8,3,128,128]{2,3,1,0:T(8,128)} fusion(bf16[512,8,3,128]{0,3,2,1:T(8,128)(2,1)} %copy.23, pred[8,3]{1,0:T(8,128)(4,1)S(1)} %copy.15, f32[8,3,128,128]{2,3,1,0:T(8,128)S(1)} %copy-done, bf16[8,3,128,128]{2,3,1,0:T(8,128)(2,1)S(1)} %copy.14, f32[]{:T(128)S(6)} %mul.61, f32[]{:T(128)S(6)} %div.29, pred[3,128,128]{1,2,0:T(8,128)(4,1)S(1)} %fusion.16), kind=kOutput, calls=%fused_computation.12 | convolution fusion | flops 813694976 | bytes 7127072 | tf_op jit(solution)/shard_map/rna,nrkb->rkab/dot_general | solution.py:32
  202.7 47.9 %all-reduce.5.cloned.1.call-done = f32[8,3,128,128]{2,3,1,0:T(8,128)} async-done(((f32[8,3,128,128]{2,3,1,0:T(8,128)}), f32[8,3,128,128]{2,3,1,0:T(8,128)}) %all-reduce.5.cloned.1.call-update) | async-done | bytes 1572880 | tf_op jit(solution)/shard_map/psum | solution.py:70
  250.6 2.6 multiply_reduce_fusion
  253.2 33.8 %psum.31 = f32[]{:T(128)} all-reduce(f32[]{:T(128)} %multiply_reduce_fusion), channel_id=1, replica_groups=mesh['var'=16,'samp'=2] {'var'}, use_global_device_ids=true, to_apply=%region_5.6 | all-reduce | flops 1 | bytes 8 | tf_op jit(solution)/shard_map/psum | solution.py:71
  287.6 2.1 multiply_subtract_fusion
  290.1 1.1 copy.27
  (27 shorter events, 1.3 us)
Async XLA Ops:
  6.5 9.4 %copy-start.4 = (s32[8,3]{0,1:T(4,128)S(1)}, s32[8,3]{0,1:T(4,128)}, u32[]{:S(2)}) copy-start(s32[8,3]{0,1:T(4,128)} %param.4) | copy-start | bytes 292
  6.5 152.0 %all-reduce.3.cloned.1.call-start = ((), (), s32[]{:S(2)}) async-start(), calls=%async_computation | async-start | bytes 3145728 | tf_op jit(solution)/shard_map/psum | solution.py:70
  8.1 60.3 %collective-permute-start = (bf16[512,1024]{0,1:T(8,128)(2,1)S(1)}, bf16[512,1024]{0,1:T(8,128)(2,1)}, u32[]{:S(2)}, u32[]{:S(2)}) collective-permute-start(bf16[512,1024]{0,1:T(8,128)(2,1)S(1)} %copy.16), channel_id=1, source_target_pairs={{28,0},{30,2},{0,4},{2,6},{4,8},{6,10},{8,12},{10,14},{12,16},{14,... | collective-permute-start | bytes 3145736 | tf_op jit(solution)/shard_map/ppermute | solution.py:17
  11.0 59.6 %collective-permute-start.1 = (bf16[512,1024]{0,1:T(8,128)(2,1)S(1)}, bf16[512,1024]{0,1:T(8,128)(2,1)}, u32[]{:S(2)}, u32[]{:S(2)}) collective-permute-start(bf16[512,1024]{0,1:T(8,128)(2,1)S(1)} %copy.16), channel_id=1, source_target_pairs={{30,0},{0,2},{2,4},{4,6},{6,8},{8,10},{10,12},{12,14},{14,16},{16,... | collective-permute-start | bytes 3145736 | tf_op jit(solution)/shard_map/ppermute | solution.py:17
  11.0 62.9 %collective-permute-start.2 = (bf16[512,1024]{0,1:T(8,128)(2,1)S(1)}, bf16[512,1024]{0,1:T(8,128)(2,1)S(1)}, u32[]{:S(2)}, u32[]{:S(2)}) collective-permute-start(bf16[512,1024]{0,1:T(8,128)(2,1)S(1)} %copy.16), channel_id=1, source_target_pairs={{2,0},{4,2},{6,4},{8,6},{10,8},{12,10},{14,12},{16,14},{18,16},{20... | collective-permute-start | bytes 3145736 | tf_op jit(solution)/shard_map/ppermute | solution.py:17
  15.5 66.7 %collective-permute-start.3 = (bf16[512,1024]{0,1:T(8,128)(2,1)S(1)}, bf16[512,1024]{0,1:T(8,128)(2,1)S(1)}, u32[]{:S(2)}, u32[]{:S(2)}) collective-permute-start(bf16[512,1024]{0,1:T(8,128)(2,1)S(1)} %copy.16), channel_id=1, source_target_pairs={{4,0},{6,2},{8,4},{10,6},{12,8},{14,10},{16,12},{18,14},{20,16},{2... | collective-permute-start | bytes 3145736 | tf_op jit(solution)/shard_map/ppermute | solution.py:17
  103.8 57.2 %copy-start.3 = (bf16[8,3,128,128]{3,2,1,0:T(8,128)(2,1)S(1)}, bf16[8,3,128,128]{3,2,1,0:T(8,128)(2,1)}, u32[]{:S(2)}) copy-start(bf16[8,3,128,128]{3,2,1,0:T(8,128)(2,1)} %param.5) | copy-start | bytes 2359300
  103.8 146.8 %all-reduce.5.cloned.1.call-start = ((), (), s32[]{:S(2)}) async-start(), calls=%async_computation.1 | async-start | bytes 3145728 | tf_op jit(solution)/shard_map/psum | solution.py:70
  158.5 37.3 %copy-start = (f32[8,3,128,128]{2,3,1,0:T(8,128)S(1)}, f32[8,3,128,128]{2,3,1,0:T(8,128)}, u32[]{:S(2)}) copy-start(f32[8,3,128,128]{2,3,1,0:T(8,128)} %all-reduce.3.cloned.1.call-done) | copy-start | bytes 4718596
  161.4 41.2 %copy-start.2 = (bf16[8,3,128,128]{2,3,1,0:T(8,128)(2,1)}, bf16[8,3,128,128]{2,3,1,0:T(8,128)(2,1)S(1)}, u32[]{:S(2)}) copy-start(bf16[8,3,128,128]{2,3,1,0:T(8,128)(2,1)S(1)} %copy.14) | copy-start | bytes 2359300
  250.6 37.0 %copy-start.1 = (f32[8,3,128,128]{2,3,1,0:T(8,128)S(1)}, f32[8,3,128,128]{2,3,1,0:T(8,128)}, u32[]{:S(2)}) copy-start(f32[8,3,128,128]{2,3,1,0:T(8,128)} %all-reduce.5.cloned.1.call-done) | copy-start | bytes 4718596
Sparse Core Ops, SparseCore 0:
  104.0 54.4 all-reduce.2
  202.8 47.7 all-reduce.4
where the time goes:
time: 299 us; the launch traced here: 298 us
  waiting for transfers between devices  162 us (54%)
  blocking collectives  67.6 us (23%)
  local copies, waits for them, and re-layouts  25.4 us (8%)
  between operations  14.7 us (5%)
  matrix products  13.1 us (4%)
  starting transfers between devices  7.89 us (3%)
  other arithmetic  7.71 us (3%)
    psum x2, waiting for transfers between devices, body(): grad = lax.psum(partial_grad, 'samp')  102 us
    psum x2, blocking collectives, body(): squares = lax.psum(jnp.sum(grad * grad), 'var')  67.6 us
    ppermute x4, waiting for transfers between devices, from_behind(): return lax.ppermute(block, axis, route)  59.3 us
    dot_general x2, matrix products, block_terms(): jnp.einsum('rna,nrkb->rkab', weighted, selected, preferred_element_type=j...  13.1 us
    unnamed x16, local copies, waits for them, and re-layouts  8.61 us
    reshape x1, local copies, waits for them, and re-layouts, body(): blocks = strips.reshape(sample_rows, 5 * row_blocks, block_size)  7.91 us
    ppermute x4, starting transfers between devices, from_behind(): return lax.ppermute(block, axis, route)  7.84 us
    gather x2, local copies, waits for them, and re-layouts, body(): jnp.take(blocks, slot_index, axis=1)  6.45 us
  transfers between devices with their start and end apart: 6, of which 4 were waited for; matrix products, arithmetic and copies ran while one was open for 2% of the time, Pallas kernels for 0%

commit v1 on v0

v1 whole, which is shorter than its diff:
```python
import functools

import jax
import jax.numpy as jnp
from jax import lax
from jax.experimental import pallas as pl
from jax.experimental.pallas import tpu as pltpu
from jax.sharding import PartitionSpec as P

ITERS = 2


STEP_SCALE = 0.5
THRESHOLD = 0.25
EPSILON = 1e-06
CHUNKS = 4


def kernel(
    var_count,
    samp_count,
    obs_ref,
    pattern_ref,
    omega_ref,
    out_ref,
    *scratch,
):
    strips = scratch[:CHUNKS]
    (
        chosen,
        staged,
        gram_hi,
        gram_lo,
        gram,
        iterate,
        grads,
        near,
        far,
        x_send,
        x_recv,
        own_send,
        own_recv,
        pick_send,
        pick_recv,
        near_send,
        near_recv,
        far_send,
        far_recv,
    ) = scratch[CHUNKS:]
    v = lax.axis_index("var")
    s = lax.axis_index("samp")
    row_blocks, slot_count, size, _ = omega_ref.shape
    share = row_blocks // samp_count
    depth = strips[0].shape[1]
    width = slot_count * size
    inverse = 1.0 / (obs_ref.shape[0] * samp_count)
    entries = row_blocks * slot_count * size * size * var_count
    core = lax.rem(v, 2)
    group = 4 * samp_count
    layers = var_count // 4
    place = lax.rem(v, 4) * samp_count + s
    layer = v // 4

    def device(var, samp):
        return {"var": var, "samp": samp}

    def near_peer(d):
        other = lax.rem(place + d, group)
        return device(layer * 4 + other // samp_count, lax.rem(other, samp_count))

    def far_peer(d):
        return device(lax.rem(layer + d, layers) * 4 + lax.rem(v, 4), s)

    above = lax.rem(v + 2, var_count)
    below = lax.rem(v + var_count - 2, var_count)
    mate = v + 1 - 2 * core
    outside = lax.rem(v + var_count - 2 + 4 * (lax.rem(v, 4) // 2), var_count)

    barrier = pltpu.get_barrier_semaphore()
    for d in range(1, group):
        pl.semaphore_signal(barrier, inc=1, device_id=near_peer(d), device_id_type=pl.DeviceIdType.MESH)
    for d in range(1, layers):
        pl.semaphore_signal(barrier, inc=1, device_id=far_peer(d), device_id_type=pl.DeviceIdType.MESH)
    pl.semaphore_signal(barrier, inc=1, device_id=device(outside, s), device_id_type=pl.DeviceIdType.MESH)

    own = 2 * row_blocks
    for c in range(CHUNKS):
        for b in range(row_blocks):
            strips[c][own + b] = obs_ref[c * depth : (c + 1) * depth, b * size : (b + 1) * size]
    pl.semaphore_wait(barrier, group - 1 + layers - 1 + 1)

    pending = []

    def remote(src, dst, send, recv, target):
        copy = pltpu.make_async_remote_copy(
            src_ref=src,
            dst_ref=dst,
            send_sem=send,
            recv_sem=recv,
            device_id=target,
            device_id_type=pl.DeviceIdType.MESH,
        )
        copy.start()
        pending.append(copy)
        return copy

    def strip(c, slot):
        return strips[c].at[pl.ds(slot * row_blocks, row_blocks)]

    arrivals = [None] * CHUNKS

    def send_strip(c):
        up = remote(strip(c, 2), strip(c, 0), x_send.at[c, 0], x_recv.at[c, 0], device(above, s))
        down = remote(strip(c, 2), strip(c, 4), x_send.at[c, 1], x_recv.at[c, 1], device(below, s))
        side = remote(strip(c, 2), strip(c, 1 + 2 * core), x_send.at[c, 2], x_recv.at[c, 2], device(mate, s))
        arrivals[c] = (up, down, side)

    own_copies = {}

    def send_own(c):
        for d in range(1, samp_count):
            peer = lax.rem(s + d, samp_count)
            own_copies[c, d] = remote(
                strips[c].at[pl.ds(own + peer * share, share)],
                chosen.at[d, c, 0],
                own_send.at[d, c],
                own_recv.at[d, c],
                device(v, peer),
            )

    def slot_of(row, k):
        column = pattern_ref[row, k]
        owner = column // row_blocks
        offset = lax.rem(owner - v + var_count + 2, var_count)
        return jnp.minimum(offset, 4) * row_blocks + lax.rem(column, row_blocks)

    def add_gram(d, c, first):
        def one(r, carry):
            x = jnp.concatenate([chosen[d, c, k, r] for k in range(slot_count)], axis=1)
            product = lax.dot_general(x, x, (((0,), (0,)), ((), ())), preferred_element_type=jnp.float32)
            if first:
                gram[r] = product
            else:
                gram[r] += product
            return carry

        lax.fori_loop(0, share, one, 0)

    picks = {}

    def wait_picked(c):
        for d in range(1, samp_count):
            own_copies[c, d].wait_recv()
            picks[c, d].wait_recv()
            add_gram(d, c, False)

    send_strip(0)
    send_strip(1)
    for c in range(CHUNKS):
        send_own(c)
    for c in range(CHUNKS):
        up, down, side = arrivals[c]
        first = 1 - core
        pltpu.make_async_remote_copy(
            src_ref=strip(c, 2),
            dst_ref=strip(c, 4 * first),
            send_sem=x_send.at[c, 3],
            recv_sem=x_recv.at[c, first],
            device_id=device(mate, s),
            device_id_type=pl.DeviceIdType.MESH,
        ).wait_recv()
        forward = remote(
            strip(c, 4 * first), strip(c, 3 - 2 * core), x_send.at[c, 3], x_recv.at[c, 3], device(mate, s)
        )
        pltpu.make_async_remote_copy(
            src_ref=strip(c, 2),
            dst_ref=strip(c, 4 * core),
            send_sem=x_send.at[c, 3],
            recv_sem=x_recv.at[c, core],
            device_id=device(mate, s),
            device_id_type=pl.DeviceIdType.MESH,
        ).wait_recv()
        if c + 2 < CHUNKS:
            send_strip(c + 2)
        side.wait_recv()
        forward.wait_recv()
        for d in range(1, samp_count):
            peer = lax.rem(s + d, samp_count)

            def stage(r, carry):
                for k in range(1, slot_count):
                    staged[d - 1, c, k - 1, r] = strips[c][slot_of(peer * share + r, k)]
                return carry

            lax.fori_loop(0, share, stage, 0)
            picks[c, d] = remote(
                staged.at[d - 1, c],
                chosen.at[d, c, pl.ds(1, slot_count - 1)],
                pick_send.at[d, c],
                pick_recv.at[d, c],
                device(v, peer),
            )

        def keep(r, carry):
            chosen[0, c, 0, r] = strips[c][own + s * share + r]
            for k in range(1, slot_count):
                chosen[0, c, k, r] = strips[c][slot_of(s * share + r, k)]
            return carry

        lax.fori_loop(0, share, keep, 0)
        add_gram(0, c, c == 0)
        if c > 0:
            wait_picked(c - 1)
    wait_picked(CHUNKS - 1)

    def split(r, carry):
        full = gram[r]
        high = full.astype(jnp.bfloat16)
        gram_hi[r] = high
        gram_lo[r] = (full - high.astype(jnp.float32)).astype(jnp.bfloat16)
        for k in range(slot_count):
            iterate[r, :, k * size : (k + 1) * size] = omega_ref[s * share + r, k].astype(jnp.float32)
        return carry

    lax.fori_loop(0, share, split, 0)

    rows = lax.broadcasted_iota(jnp.int32, (size, width), 0)
    columns = lax.broadcasted_iota(jnp.int32, (size, width), 1)
    diagonal = rows == columns

    for step in range(ITERS):

        def descend(r, total):
            packed = iterate[r].astype(jnp.bfloat16)
            grad = jnp.dot(packed, gram_hi[r], preferred_element_type=jnp.float32)
            grad += jnp.dot(packed, gram_lo[r], preferred_element_type=jnp.float32)
            grad *= inverse
            grads[r] = grad
            square = grad * grad
            folded = square[:, :size]
            for k in range(1, slot_count):
                folded += square[:, k * size : (k + 1) * size]
            return total + jnp.sum(folded.reshape(size // 8, 8, size), axis=0)

        near[step, 0] = lax.fori_loop(0, share, descend, jnp.zeros((8, size), jnp.float32))
        copies = [
            remote(near.at[step, 0], near.at[step, d], near_send.at[step, d], near_recv.at[step, d], near_peer(d))
            for d in range(1, group)
        ]
        for copy in copies:
            copy.wait_recv()
        total = near[step, 0]
        for d in range(1, group):
            total += near[step, d]
        far[step, 0] = total
        copies = [
            remote(far.at[step, 0], far.at[step, d], far_send.at[step, d], far_recv.at[step, d], far_peer(d))
            for d in range(1, layers)
        ]
        for copy in copies:
            copy.wait_recv()
        for d in range(1, layers):
            total += far[step, d]
        mean_sq = jnp.sum(jnp.sum(total, axis=0, keepdims=True), axis=1, keepdims=True) / entries
        step_size = STEP_SCALE / jnp.sqrt(mean_sq + EPSILON)

        def advance(r, carry):
            stepped = iterate[r] - step_size * grads[r]
            shrunk = stepped - jnp.clip(stepped, -THRESHOLD, THRESHOLD)
            lifted = 0.5 * (stepped + jnp.sqrt(stepped * stepped + 4.0 * step_size))
            value = jnp.where(diagonal, lifted, shrunk)
            if step + 1 < ITERS:
                iterate[r] = value
            else:
                for k in range(slot_count):
                    out_ref[r, k] = value[:, k * size : (k + 1) * size]
            return carry

        lax.fori_loop(0, share, advance, 0)

    for copy in pending:
        copy.wait_send()


def body(observed, pattern, omega_init):
    var_count = lax.axis_size("var")
    samp_count = lax.axis_size("samp")
    row_blocks, slot_count, size, _ = omega_init.shape
    share = row_blocks // samp_count
    depth = observed.shape[0] // CHUNKS
    width = slot_count * size
    group = 4 * samp_count
    layers = var_count // 4
    dma = pltpu.SemaphoreType.DMA
    scratch = [pltpu.VMEM((5 * row_blocks, depth, size), jnp.bfloat16) for _ in range(CHUNKS)]
    scratch += [
        pltpu.VMEM((samp_count, CHUNKS, slot_count, share, depth, size), jnp.bfloat16),
        pltpu.VMEM((samp_count - 1, CHUNKS, slot_count - 1, share, depth, size), jnp.bfloat16),
        pltpu.VMEM((share, width, width), jnp.bfloat16),
        pltpu.VMEM((share, width, width), jnp.bfloat16),
        pltpu.VMEM((share, width, width), jnp.float32),
        pltpu.VMEM((share, size, width), jnp.float32),
        pltpu.VMEM((share, size, width), jnp.float32),
        pltpu.VMEM((ITERS, group, 8, size), jnp.float32),
        pltpu.VMEM((ITERS, layers, 8, size), jnp.float32),
        dma((CHUNKS, 4)),
        dma((CHUNKS, 4)),
        dma((samp_count, CHUNKS)),
        dma((samp_count, CHUNKS)),
        dma((samp_count, CHUNKS)),
        dma((samp_count, CHUNKS)),
        dma((ITERS, group)),
        dma((ITERS, group)),
        dma((ITERS, layers)),
        dma((ITERS, layers)),
    ]
    vmem = pl.BlockSpec(memory_space=pltpu.VMEM)
    return pl.pallas_call(
        functools.partial(kernel, var_count, samp_count),
        out_shape=jax.ShapeDtypeStruct((share, slot_count, size, size), jnp.float32),
        in_specs=[vmem, pl.BlockSpec(memory_space=pltpu.SMEM), vmem],
        out_specs=vmem,
        scratch_shapes=scratch,
        compiler_params=pltpu.CompilerParams(
            collective_id=0, has_side_effects=True, vmem_limit_bytes=40 * 1024 * 1024
        ),
    )(observed, pattern, omega_init)


def solution(mesh):
    return jax.shard_map(
        body,
        mesh=mesh,
        in_specs=(P("samp", "var"), P("var", None), P("var", None, None, None)),
        out_specs=P(("var", "samp"), None, None, None),
        check_vma=False,
    )
```

time: 299 us -> 84.6 us (0.28)
  waiting for transfers between devices: 162 us -> 0 us
  Pallas kernels: 0 us -> 80.4 us
  blocking collectives: 67.6 us -> 0 us
  local copies, waits for them, and re-layouts: 25.4 us -> 3.99 us
  between operations: 14.7 us -> 0.01 us
  matrix products: 13.1 us -> 0 us
  starting transfers between devices: 7.89 us -> 0 us
  other arithmetic: 7.71 us -> 0 us
    psum x2 -> x0, waiting for transfers between devices: 102 us -> none  [body(): grad = lax.psum(partial_grad, 'samp')]
    pallas_call x0 -> x1, Pallas kernels: none -> 80.4 us  [body(): pl.pallas_call(functools.partial(kernel, var_count, samp_count), out_shap...]
    psum x2 -> x0, blocking collectives: 67.6 us -> none  [body(): squares = lax.psum(jnp.sum(grad * grad), 'var')]
    ppermute x4 -> x0, waiting for transfers between devices: 59.3 us -> none  [from_behind(): return lax.ppermute(block, axis, route)]
    dot_general x2 -> x0, matrix products: 13.1 us -> none  [block_terms(): jnp.einsum('rna,nrkb->rkab', weighted, selected, preferred_element_type=j...]
    reshape x2 -> x0, local copies, waits for them, and re-layouts: 7.99 us -> none  [the longest x1 7.91 us: body(): blocks = strips.reshape(sample_rows, 5 * row_blocks, block_size)]
    ppermute x4 -> x0, starting transfers between devices: 7.84 us -> none  [from_behind(): return lax.ppermute(block, axis, route)]
    gather x2 -> x0, local copies, waits for them, and re-layouts: 6.45 us -> none  [body(): jnp.take(blocks, slot_index, axis=1)]
  transfers between devices with their start and end apart: 6 -> 0, of which waited for: 4 -> 0; matrix products, arithmetic and copies ran while one was open for 2% -> 0% of each run, Pallas kernels for 0% -> 0%
where the time goes in v1:
time: 84.6 us; the launch traced here: 84.4 us
  Pallas kernels  80.4 us (95%)
  local copies, waits for them, and re-layouts  3.99 us (5%)
    pallas_call x1, Pallas kernels, body(): pl.pallas_call(functools.partial(kernel, var_count, samp_count), out_shap...  80.4 us
    unnamed x6, local copies, waits for them, and re-layouts  3.99 us

profile of v1, /device:TPU:0, one launch (start us, length us, event | category | flops | bytes accessed | tf_op | source)
XLA Modules:
  0.0 84.4 jit_solution(16572748000453168527)
XLA Ops:
  0.0 0.8 copy.4.pattern_ref
  0.8 0.0 copy-start
  0.8 1.2 %copy-done = bf16[512,1024]{1,0:T(8,128)(2,1)S(1)} copy-done((bf16[512,1024]{1,0:T(8,128)(2,1)S(1)}, bf16[512,1024]{1,0:T(8,128)(2,1)}, u32[]{:S(2)}) %copy-start) | copy-done | bytes 1048600
  2.0 0.0 copy-start.1
  2.0 1.1 %copy-done.1 = bf16[8,3,128,128]{3,2,1,0:T(8,128)(2,1)S(1)} copy-done((bf16[8,3,128,128]{3,2,1,0:T(8,128)(2,1)S(1)}, bf16[8,3,128,128]{3,2,1,0:T(8,128)(2,1)}, u32[]{:S(2)}) %copy-start.1) | copy-done | bytes 786456
  3.1 80.4 %shard_map.37 = f32[4,3,128,128]{3,2,1,0:T(8,128)S(1)} custom-call(bf16[512,1024]{1,0:T(8,128)(2,1)S(1)} %copy-done, s32[8,3]{1,0:T(8,128)S(1)} %copy.4.pattern_ref, bf16[8,3,128,128]{3,2,1,0:T(8,128)(2,1)S(1)} %copy-done.1), custom_call_target="tpu_custom_call" | custom-call | tf_op jit(solution)/shard_map/pallas_call | solution.py:318
  83.5 0.9 %copy.6 = f32[4,3,128,128]{3,2,1,0:T(8,128)} copy(f32[4,3,128,128]{3,2,1,0:T(8,128)S(1)} %shard_map.37) | data formatting | bytes 1572864
Async XLA Ops:
  0.8 1.2 %copy-start = (bf16[512,1024]{1,0:T(8,128)(2,1)S(1)}, bf16[512,1024]{1,0:T(8,128)(2,1)}, u32[]{:S(2)}) copy-start(bf16[512,1024]{1,0:T(8,128)(2,1)} %obs_ref.1) | copy-start | bytes 3145732
  2.0 1.1 %copy-start.1 = (bf16[8,3,128,128]{3,2,1,0:T(8,128)(2,1)S(1)}, bf16[8,3,128,128]{3,2,1,0:T(8,128)(2,1)}, u32[]{:S(2)}) copy-start(bf16[8,3,128,128]{3,2,1,0:T(8,128)(2,1)} %omega_ref.1) | copy-start | bytes 2359300

commit v2 on v1

v2 whole, which is shorter than its diff:
```python
import functools

import jax
import jax.numpy as jnp
from jax import lax
from jax.experimental import pallas as pl
from jax.experimental.pallas import tpu as pltpu
from jax.sharding import PartitionSpec as P

ITERS = 2


STEP_SCALE = 0.5
THRESHOLD = 0.25
EPSILON = 1e-06
CHUNKS = 4


def kernel(
    var_count,
    samp_count,
    obs_ref,
    pattern_ref,
    omega_ref,
    out_ref,
    *scratch,
):
    strips = scratch[:CHUNKS]
    (
        mine,
        theirs,
        staged,
        picked,
        omega,
        table,
        routes,
        gram_hi,
        gram_lo,
        gram,
        iterate,
        grads,
        near,
        far,
        load_sem,
        table_send,
        table_recv,
        x_send,
        x_recv,
        z_send,
        z_recv,
        mate_send,
        mate_recv,
        own_send,
        own_recv,
        pick_send,
        pick_recv,
        near_send,
        near_recv,
        far_send,
        far_recv,
    ) = scratch[CHUNKS:]
    v = lax.axis_index("var")
    s = lax.axis_index("samp")
    row_blocks, slot_count, size, _ = omega_ref.shape
    share = row_blocks // samp_count
    depth = strips[0].shape[1]
    half = depth * CHUNKS
    width = slot_count * size
    inverse = 1.0 / (obs_ref.shape[0] * samp_count)
    entries = row_blocks * slot_count * size * size * var_count
    core = lax.rem(v, 2)
    x = lax.rem(v, 4) // 2
    group = 4 * samp_count
    layers = var_count // 4
    place = lax.rem(v, 4) * samp_count + s
    layer = v // 4

    def device(var, samp):
        return {"var": var, "samp": samp}

    def near_peer(d):
        other = lax.rem(place + d, group)
        return device(layer * 4 + other // samp_count, lax.rem(other, samp_count))

    def far_peer(d):
        return device(lax.rem(layer + d, layers) * 4 + lax.rem(v, 4), s)

    mate = v + 1 - 2 * core
    across = v + 2 - 4 * x

    barrier = pltpu.get_barrier_semaphore()
    for d in range(1, group):
        pl.semaphore_signal(barrier, inc=1, device_id=near_peer(d), device_id_type=pl.DeviceIdType.MESH)
    for d in range(1, layers):
        pl.semaphore_signal(barrier, inc=1, device_id=far_peer(d), device_id_type=pl.DeviceIdType.MESH)

    loads = [
        pltpu.make_async_copy(obs_ref.at[:, pl.ds(b * size, size)], mine.at[b], load_sem.at[b])
        for b in range(row_blocks)
    ]
    load_table = pltpu.make_async_copy(pattern_ref, table.at[0], load_sem.at[row_blocks])
    load_omega = pltpu.make_async_copy(
        omega_ref.at[pl.ds(s * share, share)], omega, load_sem.at[row_blocks + 1]
    )
    load_table.start()
    for copy in loads:
        copy.start()
    load_omega.start()

    pending = []

    def remote(src, dst, send, recv, target):
        copy = pltpu.make_async_remote_copy(
            src_ref=src,
            dst_ref=dst,
            send_sem=send,
            recv_sem=recv,
            device_id=target,
            device_id_type=pl.DeviceIdType.MESH,
        )
        copy.start()
        pending.append(copy)
        return copy

    def strip(c, slot):
        return strips[c].at[pl.ds(slot * row_blocks, row_blocks)]

    def samples(side, c):
        return pl.ds(pl.multiple_of(side * half + c * depth, depth), depth)

    own_slot = 2 + 2 * x + core
    across_slot = 4 - 2 * x + core

    for copy in loads:
        copy.wait()
    pl.semaphore_wait(barrier, group - 1 + layers - 1)
    x_copies = [
        remote(mine.at[:, samples(1 - x, c)], strip(c, own_slot), x_send.at[c], x_recv.at[c], device(across, s))
        for c in range(CHUNKS)
    ]
    load_table.wait()
    table_copy = remote(table.at[0], table.at[1], table_send.at[0], table_recv.at[0], device(across, s))
    z_copies = []
    mate_copies = []
    for c in range(CHUNKS):
        strips[c][pl.ds(own_slot * row_blocks, row_blocks)] = mine[:, samples(x, c)]
        target = lax.rem(layer + layers - 1 + 2 * x, layers) * 4 + lax.rem(v, 4)
        z_copies.append(
            [
                remote(
                    strip(c, own_slot), strip(c, 6 - 6 * x + core), z_send.at[c, 0], z_recv.at[c, 0], device(target, s)
                )
            ]
        )
        mate_copies.append(
            [remote(strip(c, own_slot), strip(c, own_slot), mate_send.at[c, 0], mate_recv.at[c, 0], device(mate, s))]
        )
    own_copies = []
    for d in range(1, samp_count):
        peer = lax.rem(s + d, samp_count)
        own_copies.append(
            remote(mine.at[pl.ds(peer * share, share)], theirs.at[d], own_send.at[d], own_recv.at[d], device(v, peer))
        )

    def to_mate(c, kind, slot):
        mate_copies[c].append(
            remote(strip(c, slot), strip(c, slot), mate_send.at[c, kind], mate_recv.at[c, kind], device(mate, s))
        )

    def pass_on(c):
        x_copies[c].wait_recv()
        target = lax.rem(layer + layers + 1 - 2 * x, layers) * 4 + lax.rem(v, 4)
        z_copies[c].append(
            remote(strip(c, across_slot), strip(c, 6 * x + core), z_send.at[c, 1], z_recv.at[c, 1], device(target, s))
        )
        to_mate(c, 1, across_slot)

    def share_layers(c):
        for copy in z_copies[c]:
            copy.wait_recv()
        to_mate(c, 2, core)
        to_mate(c, 3, 6 + core)

    def block_of(e, row, k):
        column = routes[e, row, k]
        offset = lax.rem(column // row_blocks - layer * 4 + var_count + 2, var_count)
        return jnp.minimum(offset, 7) * row_blocks + lax.rem(column, row_blocks)

    picks = []

    def pick(c):
        for copy in mate_copies[c]:
            copy.wait_recv()
        sent = []
        for e, d in [(1, d) for d in range(samp_count)] + [(0, d) for d in range(samp_count)]:
            peer = lax.rem(s + d, samp_count)

            def stage(r, carry):
                for k in range(1, slot_count):
                    block = strips[c][block_of(e, peer * share + r, k)]
                    if e == 0 and d == 0:
                        picked[0, 0, c, k - 1, r] = block
                    else:
                        staged[e, d, c, k - 1, r] = block
                return carry

            lax.fori_loop(0, share, stage, 0)
            if e or d:
                sent.append(
                    remote(
                        staged.at[e, d, c],
                        picked.at[e, d, c],
                        pick_send.at[e, d, c],
                        pick_recv.at[e, d, c],
                        device(across if e else v, peer),
                    )
                )
        picks.append(sent)

    def add_gram(c):
        if c == 0:
            for copy in own_copies:
                copy.wait_recv()
        for copy in picks[c]:
            copy.wait_recv()

        def one(r, carry):
            parts = []
            for e in range(2):
                rows = samples(1 - x if e else x, c)
                for d in range(samp_count):
                    row_block = theirs[d, r, rows] if d else mine[s * share + r, rows]
                    parts.append(
                        jnp.concatenate([row_block] + [picked[e, d, c, k, r] for k in range(slot_count - 1)], axis=1)
                    )
            taken = jnp.concatenate(parts, axis=0)
            product = lax.dot_general(
                taken, taken, (((0,), (0,)), ((), ())), preferred_element_type=jnp.float32
            )
            if c == 0:
                gram[r] = product
            else:
                gram[r] += product
            return carry

        lax.fori_loop(0, share, one, 0)

    for turn in range(CHUNKS + 3):
        if turn < CHUNKS:
            pass_on(turn)
        if 0 <= turn - 1 < CHUNKS:
            share_layers(turn - 1)
        if turn == 1:
            table_copy.wait_recv()
            fetch = pltpu.make_async_copy(table, routes, load_sem.at[row_blocks + 2])
            fetch.start()
            fetch.wait()
        if 0 <= turn - 2 < CHUNKS:
            pick(turn - 2)
        if 0 <= turn - 3 < CHUNKS:
            add_gram(turn - 3)
    load_omega.wait()

    def split(r, carry):
        full = gram[r]
        high = full.astype(jnp.bfloat16)
        gram_hi[r] = high
        gram_lo[r] = (full - high.astype(jnp.float32)).astype(jnp.bfloat16)
        for k in range(slot_count):
            iterate[r, :, k * size : (k + 1) * size] = omega[r, k].astype(jnp.float32)
        return carry

    lax.fori_loop(0, share, split, 0)

    rows = lax.broadcasted_iota(jnp.int32, (size, width), 0)
    columns = lax.broadcasted_iota(jnp.int32, (size, width), 1)
    diagonal = rows == columns

    for step in range(ITERS):

        def descend(r, total):
            packed = iterate[r].astype(jnp.bfloat16)
            grad = jnp.dot(packed, gram_hi[r], preferred_element_type=jnp.float32)
            grad += jnp.dot(packed, gram_lo[r], preferred_element_type=jnp.float32)
            grad *= inverse
            grads[r] = grad
            square = grad * grad
            folded = square[:, :size]
            for k in range(1, slot_count):
                folded += square[:, k * size : (k + 1) * size]
            return total + jnp.sum(folded.reshape(size // 8, 8, size), axis=0)

        near[step, 0] = lax.fori_loop(0, share, descend, jnp.zeros((8, size), jnp.float32))
        copies = [
            remote(near.at[step, 0], near.at[step, d], near_send.at[step, d], near_recv.at[step, d], near_peer(d))
            for d in range(1, group)
        ]
        for copy in copies:
            copy.wait_recv()
        total = near[step, 0]
        for d in range(1, group):
            total += near[step, d]
        far[step, 0] = total
        copies = [
            remote(far.at[step, 0], far.at[step, d], far_send.at[step, d], far_recv.at[step, d], far_peer(d))
            for d in range(1, layers)
        ]
        for copy in copies:
            copy.wait_recv()
        for d in range(1, layers):
            total += far[step, d]
        mean_sq = jnp.sum(jnp.sum(total, axis=0, keepdims=True), axis=1, keepdims=True) / entries
        step_size = STEP_SCALE / jnp.sqrt(mean_sq + EPSILON)

        def advance(r, carry):
            stepped = iterate[r] - step_size * grads[r]
            shrunk = stepped - jnp.clip(stepped, -THRESHOLD, THRESHOLD)
            lifted = 0.5 * (stepped + jnp.sqrt(stepped * stepped + 4.0 * step_size))
            value = jnp.where(diagonal, lifted, shrunk)
            if step + 1 < ITERS:
                iterate[r] = value
            else:
                for k in range(slot_count):
                    out_ref[r, k] = value[:, k * size : (k + 1) * size]
            return carry

        lax.fori_loop(0, share, advance, 0)

    for copy in pending:
        copy.wait_send()


def body(observed, pattern, omega_init):
    var_count = lax.axis_size("var")
    samp_count = lax.axis_size("samp")
    row_blocks, slot_count, size, _ = omega_init.shape
    share = row_blocks // samp_count
    sample_rows = observed.shape[0]
    depth = sample_rows // (2 * CHUNKS)
    width = slot_count * size
    group = 4 * samp_count
    layers = var_count // 4
    dma = pltpu.SemaphoreType.DMA
    pattern = jnp.pad(pattern, ((0, 0), (0, size - slot_count)))
    scratch = [pltpu.VMEM((8 * row_blocks, depth, size), jnp.bfloat16) for _ in range(CHUNKS)]
    pick_shape = (2, samp_count, CHUNKS, slot_count - 1, share, depth, size)
    scratch += [
        pltpu.VMEM((row_blocks, sample_rows, size), jnp.bfloat16),
        pltpu.VMEM((samp_count, share, sample_rows, size), jnp.bfloat16),
        pltpu.VMEM(pick_shape, jnp.bfloat16),
        pltpu.VMEM(pick_shape, jnp.bfloat16),
        pltpu.VMEM((share, slot_count, size, size), jnp.bfloat16),
        pltpu.VMEM((2, row_blocks, size), jnp.int32),
        pltpu.SMEM((2, row_blocks, size), jnp.int32),
        pltpu.VMEM((share, width, width), jnp.bfloat16),
        pltpu.VMEM((share, width, width), jnp.bfloat16),
        pltpu.VMEM((share, width, width), jnp.float32),
        pltpu.VMEM((share, size, width), jnp.float32),
        pltpu.VMEM((share, size, width), jnp.float32),
        pltpu.VMEM((ITERS, group, 8, size), jnp.float32),
        pltpu.VMEM((ITERS, layers, 8, size), jnp.float32),
        dma((row_blocks + 3,)),
        dma((1,)),
        dma((1,)),
        dma((CHUNKS,)),
        dma((CHUNKS,)),
        dma((CHUNKS, 2)),
        dma((CHUNKS, 2)),
        dma((CHUNKS, 4)),
        dma((CHUNKS, 4)),
        dma((samp_count,)),
        dma((samp_count,)),
        dma((2, samp_count, CHUNKS)),
        dma((2, samp_count, CHUNKS)),
        dma((ITERS, group)),
        dma((ITERS, group)),
        dma((ITERS, layers)),
        dma((ITERS, layers)),
    ]
    hbm = pl.BlockSpec(memory_space=pl.ANY)
    return pl.pallas_call(
        functools.partial(kernel, var_count, samp_count),
        out_shape=jax.ShapeDtypeStruct((share, slot_count, size, size), jnp.float32),
        in_specs=[hbm, hbm, hbm],
        out_specs=pl.BlockSpec(memory_space=pltpu.VMEM),
        scratch_shapes=scratch,
        compiler_params=pltpu.CompilerParams(
            collective_id=0, has_side_effects=True, vmem_limit_bytes=56 * 1024 * 1024
        ),
    )(observed, pattern, omega_init)


def solution(mesh):
    return jax.shard_map(
        body,
        mesh=mesh,
        in_specs=(P("samp", "var"), P("var", None), P("var", None, None, None)),
        out_specs=P(("var", "samp"), None, None, None),
        check_vma=False,
    )
```

time: 84.6 us -> 73.8 us (0.87)
  Pallas kernels: 80.4 us -> 70.2 us
    pallas_call x1, Pallas kernels: 80.4 us -> 70.2 us  [body(): pl.pallas_call(functools.partial(kernel, var_count, samp_count), out_shap...]
    unnamed x6 -> x2, local copies, waits for them, and re-layouts: 3.99 us -> 2.82 us
where the time goes in v2:
time: 73.8 us; the launch traced here: 73.6 us
  Pallas kernels  70.2 us (95%)
  local copies, waits for them, and re-layouts  3.42 us (5%)
    pallas_call x1, Pallas kernels, body(): pl.pallas_call(functools.partial(kernel, var_count, samp_count), out_shap...  70.2 us
    unnamed x2, local copies, waits for them, and re-layouts  2.82 us

profile of v2, /device:TPU:0, one launch (start us, length us, event | category | flops | bytes accessed | tf_op | source)
XLA Modules:
  0.0 73.6 jit_solution(3643637830546466153)
XLA Ops:
  0.0 0.8 %copy.4 = s32[8,3]{1,0:T(8,128)S(1)} copy(s32[8,3]{0,1:T(4,128)} %param.4) | data formatting | bytes 192 | tf_op args[1]
  0.8 0.6 pad.4.pattern_ref
  1.4 70.2 %shard_map.37 = f32[4,3,128,128]{3,2,1,0:T(8,128)} custom-call(bf16[512,1024]{1,0:T(8,128)(2,1)} %obs_ref.1, s32[8,128]{1,0:T(8,128)} %pad.4.pattern_ref, bf16[8,3,128,128]{3,2,1,0:T(8,128)(2,1)} %omega_ref.1), custom_call_target="tpu_custom_call" | custom-call | tf_op jit(solution)/shard_map/pallas_call | solution.py:381
  71.5 2.1 %copy.6 = f32[4,3,128,128]{3,2,1,0:T(8,128)} copy(f32[4,3,128,128]{3,2,1,0:T(8,128)} %shard_map.37) | data formatting | bytes 1572864

commit v3 on v2

--- a/solution.py
+++ b/solution.py
@@ -134,15 +134,14 @@
     for copy in loads:
         copy.wait()
     pl.semaphore_wait(barrier, group - 1 + layers - 1)
-    x_copies = [
-        remote(mine.at[:, samples(1 - x, c)], strip(c, own_slot), x_send.at[c], x_recv.at[c], device(across, s))
-        for c in range(CHUNKS)
-    ]
-    load_table.wait()
-    table_copy = remote(table.at[0], table.at[1], table_send.at[0], table_recv.at[0], device(across, s))
+    x_copies = []
     z_copies = []
     mate_copies = []
-    for c in range(CHUNKS):
+
+    def begin(c):
+        x_copies.append(
+            remote(mine.at[:, samples(1 - x, c)], strip(c, own_slot), x_send.at[c], x_recv.at[c], device(across, s))
+        )
         strips[c][pl.ds(own_slot * row_blocks, row_blocks)] = mine[:, samples(x, c)]
         target = lax.rem(layer + layers - 1 + 2 * x, layers) * 4 + lax.rem(v, 4)
         z_copies.append(
@@ -155,6 +154,11 @@
         mate_copies.append(
             [remote(strip(c, own_slot), strip(c, own_slot), mate_send.at[c, 0], mate_recv.at[c, 0], device(mate, s))]
         )
+
+    begin(0)
+    begin(1)
+    load_table.wait()
+    table_copy = remote(table.at[0], table.at[1], table_send.at[0], table_recv.at[0], device(across, s))
     own_copies = []
     for d in range(1, samp_count):
         peer = lax.rem(s + d, samp_count)
@@ -174,6 +178,8 @@
             remote(strip(c, across_slot), strip(c, 6 * x + core), z_send.at[c, 1], z_recv.at[c, 1], device(target, s))
         )
         to_mate(c, 1, across_slot)
+        if c + 2 < CHUNKS:
+            begin(c + 2)
 
     def share_layers(c):
         for copy in z_copies[c]:
@@ -182,7 +188,7 @@
         to_mate(c, 3, 6 + core)
 
     def block_of(e, row, k):
-        column = routes[e, row, k]
+        column = routes[e, k, row]
         offset = lax.rem(column // row_blocks - layer * 4 + var_count + 2, var_count)
         return jnp.minimum(offset, 7) * row_blocks + lax.rem(column, row_blocks)
 
@@ -341,7 +347,7 @@
     group = 4 * samp_count
     layers = var_count // 4
     dma = pltpu.SemaphoreType.DMA
-    pattern = jnp.pad(pattern, ((0, 0), (0, size - slot_count)))
+    pattern = pattern.T
     scratch = [pltpu.VMEM((8 * row_blocks, depth, size), jnp.bfloat16) for _ in range(CHUNKS)]
     pick_shape = (2, samp_count, CHUNKS, slot_count - 1, share, depth, size)
     scratch += [
@@ -350,8 +356,8 @@
         pltpu.VMEM(pick_shape, jnp.bfloat16),
         pltpu.VMEM(pick_shape, jnp.bfloat16),
         pltpu.VMEM((share, slot_count, size, size), jnp.bfloat16),
-        pltpu.VMEM((2, row_blocks, size), jnp.int32),
-        pltpu.SMEM((2, row_blocks, size), jnp.int32),
+        pltpu.VMEM((2, slot_count, row_blocks), jnp.int32),
+        pltpu.SMEM((2, slot_count, row_blocks), jnp.int32),
         pltpu.VMEM((share, width, width), jnp.bfloat16),
         pltpu.VMEM((share, width, width), jnp.bfloat16),
         pltpu.VMEM((share, width, width), jnp.float32),
@@ -377,7 +383,7 @@
         dma((ITERS, layers)),
         dma((ITERS, layers)),
     ]
-    hbm = pl.BlockSpec(memory_space=pl.ANY)
+    hbm = pl.BlockSpec(memory_space=pltpu.HBM)
     return pl.pallas_call(
         functools.partial(kernel, var_count, samp_count),
         out_shape=jax.ShapeDtypeStruct((share, slot_count, size, size), jnp.float32),
@@ -385,7 +391,7 @@
         out_specs=pl.BlockSpec(memory_space=pltpu.VMEM),
         scratch_shapes=scratch,
         compiler_params=pltpu.CompilerParams(
-            collective_id=0, has_side_effects=True, vmem_limit_bytes=56 * 1024 * 1024
+            collective_id=0, has_side_effects=True, vmem_limit_bytes=53 * 1024 * 1024
         ),
     )(observed, pattern, omega_init)
 

time: 73.8 us -> 68.8 us (0.932)
  Pallas kernels: 70.2 us -> 67 us
  local copies, waits for them, and re-layouts: 3.42 us -> 1.56 us
    pallas_call x1, Pallas kernels: 70.2 us -> 67 us  [body(): pl.pallas_call(functools.partial(kernel, var_count, samp_count), out_shap...]
    unnamed x2 -> x3, local copies, waits for them, and re-layouts: 2.82 us -> 1.56 us
where the time goes in v3:
time: 68.8 us; the launch traced here: 68.6 us
  Pallas kernels  67 us (97%)
  local copies, waits for them, and re-layouts  1.56 us (2%)
    pallas_call x1, Pallas kernels, body(): pl.pallas_call(functools.partial(kernel, var_count, samp_count), out_shap...  67 us
    unnamed x3, local copies, waits for them, and re-layouts  1.56 us

profile of v3, /device:TPU:0, one launch (start us, length us, event | category | flops | bytes accessed | tf_op | source)
XLA Modules:
  0.0 68.6 jit_solution(11875628265167783857)
XLA Ops:
  0.0 0.0 copy-start
  0.0 0.7 copy-done
  0.7 67.0 %shard_map.37 = f32[4,3,128,128]{3,2,1,0:T(8,128)S(1)} custom-call(bf16[512,1024]{1,0:T(8,128)(2,1)} %obs_ref.1, s32[3,8]{1,0:T(4,128)S(1)} %bitcast.1, bf16[8,3,128,128]{3,2,1,0:T(8,128)(2,1)} %omega_ref.1), custom_call_target="tpu_custom_call" | custom-call | tf_op jit(solution)/shard_map/pallas_call | solution.py:387
  67.7 0.9 %copy.5 = f32[4,3,128,128]{3,2,1,0:T(8,128)} copy(f32[4,3,128,128]{3,2,1,0:T(8,128)S(1)} %shard_map.37) | data formatting | bytes 1572864
Async XLA Ops:
  0.0 0.7 copy-start

commit v4 on v3

--- a/solution.py
+++ b/solution.py
@@ -13,7 +13,8 @@
 STEP_SCALE = 0.5
 THRESHOLD = 0.25
 EPSILON = 1e-06
-CHUNKS = 4
+CHUNKS = 8
+AHEAD = 3
 
 
 def kernel(
@@ -34,6 +35,7 @@
         omega,
         table,
         routes,
+        slots,
         gram_hi,
         gram_lo,
         gram,
@@ -155,8 +157,8 @@
             [remote(strip(c, own_slot), strip(c, own_slot), mate_send.at[c, 0], mate_recv.at[c, 0], device(mate, s))]
         )
 
-    begin(0)
-    begin(1)
+    for c in range(AHEAD):
+        begin(c)
     load_table.wait()
     table_copy = remote(table.at[0], table.at[1], table_send.at[0], table_recv.at[0], device(across, s))
     own_copies = []
@@ -178,8 +180,8 @@
             remote(strip(c, across_slot), strip(c, 6 * x + core), z_send.at[c, 1], z_recv.at[c, 1], device(target, s))
         )
         to_mate(c, 1, across_slot)
-        if c + 2 < CHUNKS:
-            begin(c + 2)
+        if c + AHEAD < CHUNKS:
+            begin(c + AHEAD)
 
     def share_layers(c):
         for copy in z_copies[c]:
@@ -200,17 +202,13 @@
         sent = []
         for e, d in [(1, d) for d in range(samp_count)] + [(0, d) for d in range(samp_count)]:
             peer = lax.rem(s + d, samp_count)
-
-            def stage(r, carry):
+            for r in range(share):
                 for k in range(1, slot_count):
-                    block = strips[c][block_of(e, peer * share + r, k)]
+                    block = strips[c][slots[e, d, k, r]]
                     if e == 0 and d == 0:
                         picked[0, 0, c, k - 1, r] = block
                     else:
                         staged[e, d, c, k - 1, r] = block
-                return carry
-
-            lax.fori_loop(0, share, stage, 0)
             if e or d:
                 sent.append(
                     remote(
@@ -249,9 +247,9 @@
                 gram[r] += product
             return carry
 
-        lax.fori_loop(0, share, one, 0)
-
-    for turn in range(CHUNKS + 3):
+        lax.fori_loop(0, share, one, 0, unroll=True)
+
+    for turn in range(CHUNKS + 4):
         if turn < CHUNKS:
             pass_on(turn)
         if 0 <= turn - 1 < CHUNKS:
@@ -261,10 +259,15 @@
             fetch = pltpu.make_async_copy(table, routes, load_sem.at[row_blocks + 2])
             fetch.start()
             fetch.wait()
+            for e in range(2):
+                for d in range(samp_count):
+                    for k in range(1, slot_count):
+                        for r in range(share):
+                            slots[e, d, k, r] = block_of(e, lax.rem(s + d, samp_count) * share + r, k)
         if 0 <= turn - 2 < CHUNKS:
             pick(turn - 2)
-        if 0 <= turn - 3 < CHUNKS:
-            add_gram(turn - 3)
+        if 0 <= turn - 4 < CHUNKS:
+            add_gram(turn - 4)
     load_omega.wait()
 
     def split(r, carry):
@@ -276,10 +279,10 @@
             iterate[r, :, k * size : (k + 1) * size] = omega[r, k].astype(jnp.float32)
         return carry
 
-    lax.fori_loop(0, share, split, 0)
-
-    rows = lax.broadcasted_iota(jnp.int32, (size, width), 0)
-    columns = lax.broadcasted_iota(jnp.int32, (size, width), 1)
+    lax.fori_loop(0, share, split, 0, unroll=True)
+
+    rows = lax.broadcasted_iota(jnp.int32, (size, size), 0)
+    columns = lax.broadcasted_iota(jnp.int32, (size, size), 1)
     diagonal = rows == columns
 
     for step in range(ITERS):
@@ -296,7 +299,9 @@
                 folded += square[:, k * size : (k + 1) * size]
             return total + jnp.sum(folded.reshape(size // 8, 8, size), axis=0)
 
-        near[step, 0] = lax.fori_loop(0, share, descend, jnp.zeros((8, size), jnp.float32))
+        near[step, 0] = lax.fori_loop(
+            0, share, descend, jnp.zeros((8, size), jnp.float32), unroll=True
+        )
         copies = [
             remote(near.at[step, 0], near.at[step, d], near_send.at[step, d], near_recv.at[step, d], near_peer(d))
             for d in range(1, group)
@@ -319,18 +324,20 @@
         step_size = STEP_SCALE / jnp.sqrt(mean_sq + EPSILON)
 
         def advance(r, carry):
-            stepped = iterate[r] - step_size * grads[r]
-            shrunk = stepped - jnp.clip(stepped, -THRESHOLD, THRESHOLD)
-            lifted = 0.5 * (stepped + jnp.sqrt(stepped * stepped + 4.0 * step_size))
-            value = jnp.where(diagonal, lifted, shrunk)
-            if step + 1 < ITERS:
-                iterate[r] = value
-            else:
-                for k in range(slot_count):
-                    out_ref[r, k] = value[:, k * size : (k + 1) * size]
+            for k in range(slot_count):
+                lanes = slice(k * size, (k + 1) * size)
+                stepped = iterate[r, :, lanes] - step_size * grads[r, :, lanes]
+                value = stepped - jnp.clip(stepped, -THRESHOLD, THRESHOLD)
+                if k == 0:
+                    lifted = 0.5 * (stepped + jnp.sqrt(stepped * stepped + 4.0 * step_size))
+                    value = jnp.where(diagonal, lifted, value)
+                if step + 1 < ITERS:
+                    iterate[r, :, lanes] = value
+                else:
+                    out_ref[r, k] = value
             return carry
 
-        lax.fori_loop(0, share, advance, 0)
+        lax.fori_loop(0, share, advance, 0, unroll=True)
 
     for copy in pending:
         copy.wait_send()
@@ -358,6 +365,7 @@
         pltpu.VMEM((share, slot_count, size, size), jnp.bfloat16),
         pltpu.VMEM((2, slot_count, row_blocks), jnp.int32),
         pltpu.SMEM((2, slot_count, row_blocks), jnp.int32),
+        pltpu.SMEM((2, samp_count, slot_count, share), jnp.int32),
         pltpu.VMEM((share, width, width), jnp.bfloat16),
         pltpu.VMEM((share, width, width), jnp.bfloat16),
         pltpu.VMEM((share, width, width), jnp.float32),

time: 68.8 us -> 64.4 us (0.936)
  Pallas kernels: 67 us -> 62.7 us
    pallas_call x1, Pallas kernels: 67 us -> 62.7 us  [body(): pl.pallas_call(functools.partial(kernel, var_count, samp_count), out_shap...]
where the time goes in v4:
time: 64.4 us; the launch traced here: 64.3 us
  Pallas kernels  62.7 us (97%)
  local copies, waits for them, and re-layouts  1.56 us (2%)
    pallas_call x1, Pallas kernels, body(): pl.pallas_call(functools.partial(kernel, var_count, samp_count), out_shap...  62.7 us
    unnamed x3, local copies, waits for them, and re-layouts  1.56 us

profile of v4, /device:TPU:0, one launch (start us, length us, event | category | flops | bytes accessed | tf_op | source)
XLA Modules:
  0.0 64.3 jit_solution(7906685448930536746)
XLA Ops:
  0.0 0.0 copy-start
  0.0 0.7 %copy-done = s32[8,3]{0,1:T(4,128)S(1)} copy-done((s32[8,3]{0,1:T(4,128)S(1)}, s32[8,3]{0,1:T(4,128)}, u32[]{:S(2)}) %copy-start) | copy-done | bytes 120
  0.7 62.7 %shard_map.37 = f32[4,3,128,128]{3,2,1,0:T(8,128)S(1)} custom-call(bf16[512,1024]{1,0:T(8,128)(2,1)} %obs_ref.1, s32[3,8]{1,0:T(4,128)S(1)} %bitcast.1, bf16[8,3,128,128]{3,2,1,0:T(8,128)(2,1)} %omega_ref.1), custom_call_target="tpu_custom_call" | custom-call | tf_op jit(solution)/shard_map/pallas_call | solution.py:395
  63.4 0.9 %copy.5 = f32[4,3,128,128]{3,2,1,0:T(8,128)} copy(f32[4,3,128,128]{3,2,1,0:T(8,128)S(1)} %shard_map.37) | data formatting | bytes 1572864
Async XLA Ops:
  0.0 0.7 %copy-start = (s32[8,3]{0,1:T(4,128)S(1)}, s32[8,3]{0,1:T(4,128)}, u32[]{:S(2)}) copy-start(s32[8,3]{0,1:T(4,128)} %param.4) | copy-start | bytes 292

commit v5 on v4

--- a/solution.py
+++ b/solution.py
@@ -14,7 +14,7 @@
 THRESHOLD = 0.25
 EPSILON = 1e-06
 CHUNKS = 8
-AHEAD = 3
+AHEAD = 4
 
 
 def kernel(
@@ -241,19 +241,24 @@
             product = lax.dot_general(
                 taken, taken, (((0,), (0,)), ((), ())), preferred_element_type=jnp.float32
             )
+            packed = jnp.concatenate([omega[r, k] for k in range(slot_count)], axis=1)
+            weighted = lax.dot_general(
+                packed, taken, (((1,), (1,)), ((), ())), preferred_element_type=jnp.float32
+            ).astype(jnp.bfloat16)
+            grad = jnp.dot(weighted, taken, preferred_element_type=jnp.float32)
             if c == 0:
                 gram[r] = product
+                grads[r] = grad
             else:
                 gram[r] += product
+                grads[r] += grad
             return carry
 
         lax.fori_loop(0, share, one, 0, unroll=True)
 
-    for turn in range(CHUNKS + 4):
+    for turn in range(CHUNKS + 5):
         if turn < CHUNKS:
             pass_on(turn)
-        if 0 <= turn - 1 < CHUNKS:
-            share_layers(turn - 1)
         if turn == 1:
             table_copy.wait_recv()
             fetch = pltpu.make_async_copy(table, routes, load_sem.at[row_blocks + 2])
@@ -264,11 +269,13 @@
                     for k in range(1, slot_count):
                         for r in range(share):
                             slots[e, d, k, r] = block_of(e, lax.rem(s + d, samp_count) * share + r, k)
+            load_omega.wait()
         if 0 <= turn - 2 < CHUNKS:
-            pick(turn - 2)
-        if 0 <= turn - 4 < CHUNKS:
-            add_gram(turn - 4)
-    load_omega.wait()
+            share_layers(turn - 2)
+        if 0 <= turn - 3 < CHUNKS:
+            pick(turn - 3)
+        if 0 <= turn - 5 < CHUNKS:
+            add_gram(turn - 5)
 
     def split(r, carry):
         full = gram[r]
@@ -279,8 +286,6 @@
             iterate[r, :, k * size : (k + 1) * size] = omega[r, k].astype(jnp.float32)
         return carry
 
-    lax.fori_loop(0, share, split, 0, unroll=True)
-
     rows = lax.broadcasted_iota(jnp.int32, (size, size), 0)
     columns = lax.broadcasted_iota(jnp.int32, (size, size), 1)
     diagonal = rows == columns
@@ -288,9 +293,12 @@
     for step in range(ITERS):
 
         def descend(r, total):
-            packed = iterate[r].astype(jnp.bfloat16)
-            grad = jnp.dot(packed, gram_hi[r], preferred_element_type=jnp.float32)
-            grad += jnp.dot(packed, gram_lo[r], preferred_element_type=jnp.float32)
+            if step == 0:
+                grad = grads[r]
+            else:
+                packed = iterate[r].astype(jnp.bfloat16)
+                grad = jnp.dot(packed, gram_hi[r], preferred_element_type=jnp.float32)
+                grad += jnp.dot(packed, gram_lo[r], preferred_element_type=jnp.float32)
             grad *= inverse
             grads[r] = grad
             square = grad * grad
@@ -306,6 +314,8 @@
             remote(near.at[step, 0], near.at[step, d], near_send.at[step, d], near_recv.at[step, d], near_peer(d))
             for d in range(1, group)
         ]
+        if step == 0:
+            lax.fori_loop(0, share, split, 0, unroll=True)
         for copy in copies:
             copy.wait_recv()
         total = near[step, 0]

time: 64.4 us -> 63 us (0.978)
  Pallas kernels: 62.7 us -> 61.3 us
    pallas_call x1, Pallas kernels: 62.7 us -> 61.3 us  [body(): pl.pallas_call(functools.partial(kernel, var_count, samp_count), out_shap...]
where the time goes in v5:
time: 63 us; the launch traced here: 62.9 us
  Pallas kernels  61.3 us (97%)
  local copies, waits for them, and re-layouts  1.56 us (2%)
    pallas_call x1, Pallas kernels, body(): pl.pallas_call(functools.partial(kernel, var_count, samp_count), out_shap...  61.3 us
    unnamed x3, local copies, waits for them, and re-layouts  1.56 us

profile of v5, /device:TPU:0, one launch (start us, length us, event | category | flops | bytes accessed | tf_op | source)
XLA Modules:
  0.0 62.9 jit_solution(13624209014178621753)
XLA Ops:
  0.0 0.0 copy-start
  0.0 0.7 %copy-done = s32[8,3]{0,1:T(4,128)S(1)} copy-done((s32[8,3]{0,1:T(4,128)S(1)}, s32[8,3]{0,1:T(4,128)}, u32[]{:S(2)}) %copy-start) | copy-done | bytes 120
  0.7 61.3 %shard_map.37 = f32[4,3,128,128]{3,2,1,0:T(8,128)S(1)} custom-call(bf16[512,1024]{1,0:T(8,128)(2,1)} %obs_ref.1, s32[3,8]{1,0:T(4,128)S(1)} %bitcast.1, bf16[8,3,128,128]{3,2,1,0:T(8,128)(2,1)} %omega_ref.1), custom_call_target="tpu_custom_call" | custom-call | tf_op jit(solution)/shard_map/pallas_call | solution.py:405
  62.0 0.9 %copy.5 = f32[4,3,128,128]{3,2,1,0:T(8,128)} copy(f32[4,3,128,128]{3,2,1,0:T(8,128)S(1)} %shard_map.37) | data formatting | bytes 1572864
Async XLA Ops:
  0.0 0.7 %copy-start = (s32[8,3]{0,1:T(4,128)S(1)}, s32[8,3]{0,1:T(4,128)}, u32[]{:S(2)}) copy-start(s32[8,3]{0,1:T(4,128)} %param.4) | copy-start | bytes 292

commit v6 on v5

--- a/solution.py
+++ b/solution.py
@@ -130,8 +130,8 @@
     def samples(side, c):
         return pl.ds(pl.multiple_of(side * half + c * depth, depth), depth)
 
-    own_slot = 2 + 2 * x + core
-    across_slot = 4 - 2 * x + core
+    own_slot = core * 4 + 1 + x
+    across_slot = core * 4 + 2 - x
 
     for copy in loads:
         copy.wait()
@@ -149,12 +149,9 @@
         z_copies.append(
             [
                 remote(
-                    strip(c, own_slot), strip(c, 6 - 6 * x + core), z_send.at[c, 0], z_recv.at[c, 0], device(target, s)
+                    strip(c, own_slot), strip(c, core * 4 + 3 - 3 * x), z_send.at[c, 0], z_recv.at[c, 0], device(target, s)
                 )
             ]
-        )
-        mate_copies.append(
-            [remote(strip(c, own_slot), strip(c, own_slot), mate_send.at[c, 0], mate_recv.at[c, 0], device(mate, s))]
         )
 
     for c in range(AHEAD):
@@ -168,39 +165,33 @@
             remote(mine.at[pl.ds(peer * share, share)], theirs.at[d], own_send.at[d], own_recv.at[d], device(v, peer))
         )
 
-    def to_mate(c, kind, slot):
-        mate_copies[c].append(
-            remote(strip(c, slot), strip(c, slot), mate_send.at[c, kind], mate_recv.at[c, kind], device(mate, s))
-        )
-
     def pass_on(c):
         x_copies[c].wait_recv()
         target = lax.rem(layer + layers + 1 - 2 * x, layers) * 4 + lax.rem(v, 4)
         z_copies[c].append(
-            remote(strip(c, across_slot), strip(c, 6 * x + core), z_send.at[c, 1], z_recv.at[c, 1], device(target, s))
-        )
-        to_mate(c, 1, across_slot)
+            remote(strip(c, across_slot), strip(c, core * 4 + 3 * x), z_send.at[c, 1], z_recv.at[c, 1], device(target, s))
+        )
         if c + AHEAD < CHUNKS:
             begin(c + AHEAD)
 
     def share_layers(c):
         for copy in z_copies[c]:
             copy.wait_recv()
-        to_mate(c, 2, core)
-        to_mate(c, 3, 6 + core)
+        all_mine = strips[c].at[pl.ds(core * 4 * row_blocks, 4 * row_blocks)]
+        mate_copies.append(remote(all_mine, all_mine, mate_send.at[c], mate_recv.at[c], device(mate, s)))
 
     def block_of(e, row, k):
         column = routes[e, k, row]
         offset = lax.rem(column // row_blocks - layer * 4 + var_count + 2, var_count)
-        return jnp.minimum(offset, 7) * row_blocks + lax.rem(column, row_blocks)
+        offset = jnp.minimum(offset, 7)
+        return (lax.rem(offset, 2) * 4 + offset // 2) * row_blocks + lax.rem(column, row_blocks)
 
     picks = []
 
     def pick(c):
-        for copy in mate_copies[c]:
-            copy.wait_recv()
+        mate_copies[c].wait_recv()
         sent = []
-        for e, d in [(1, d) for d in range(samp_count)] + [(0, d) for d in range(samp_count)]:
+        for e, d in [(1 - e, samp_count - 1 - d) for e in range(2) for d in range(samp_count)]:
             peer = lax.rem(s + d, samp_count)
             for r in range(share):
                 for k in range(1, slot_count):
@@ -221,40 +212,45 @@
                 )
         picks.append(sent)
 
-    def add_gram(c):
+    def take(c, r):
+        parts = []
+        for e in range(2):
+            rows = samples(1 - x if e else x, c)
+            for d in range(samp_count):
+                row_block = theirs[d, r, rows] if d else mine[s * share + r, rows]
+                parts.append(
+                    jnp.concatenate([row_block] + [picked[e, d, c, k, r] for k in range(slot_count - 1)], axis=1)
+                )
+        return jnp.concatenate(parts, axis=0)
+
+    def add_grad(c):
         if c == 0:
             for copy in own_copies:
                 copy.wait_recv()
         for copy in picks[c]:
             copy.wait_recv()
-
-        def one(r, carry):
-            parts = []
-            for e in range(2):
-                rows = samples(1 - x if e else x, c)
-                for d in range(samp_count):
-                    row_block = theirs[d, r, rows] if d else mine[s * share + r, rows]
-                    parts.append(
-                        jnp.concatenate([row_block] + [picked[e, d, c, k, r] for k in range(slot_count - 1)], axis=1)
-                    )
-            taken = jnp.concatenate(parts, axis=0)
-            product = lax.dot_general(
-                taken, taken, (((0,), (0,)), ((), ())), preferred_element_type=jnp.float32
-            )
+        for r in range(share):
+            taken = take(c, r)
             packed = jnp.concatenate([omega[r, k] for k in range(slot_count)], axis=1)
             weighted = lax.dot_general(
                 packed, taken, (((1,), (1,)), ((), ())), preferred_element_type=jnp.float32
             ).astype(jnp.bfloat16)
             grad = jnp.dot(weighted, taken, preferred_element_type=jnp.float32)
             if c == 0:
-                gram[r] = product
                 grads[r] = grad
             else:
+                grads[r] += grad
+
+    def add_gram(c):
+        for r in range(share):
+            taken = take(c, r)
+            product = lax.dot_general(
+                taken, taken, (((0,), (0,)), ((), ())), preferred_element_type=jnp.float32
+            )
+            if c == 0:
+                gram[r] = product
+            else:
                 gram[r] += product
-                grads[r] += grad
-            return carry
-
-        lax.fori_loop(0, share, one, 0, unroll=True)
 
     for turn in range(CHUNKS + 5):
         if turn < CHUNKS:
@@ -275,7 +271,9 @@
         if 0 <= turn - 3 < CHUNKS:
             pick(turn - 3)
         if 0 <= turn - 5 < CHUNKS:
-            add_gram(turn - 5)
+            add_grad(turn - 5)
+            if turn - 5 < CHUNKS - 1:
+                add_gram(turn - 5)
 
     def split(r, carry):
         full = gram[r]
@@ -315,6 +313,7 @@
             for d in range(1, group)
         ]
         if step == 0:
+            add_gram(CHUNKS - 1)
             lax.fori_loop(0, share, split, 0, unroll=True)
         for copy in copies:
             copy.wait_recv()
@@ -390,8 +389,8 @@
         dma((CHUNKS,)),
         dma((CHUNKS, 2)),
         dma((CHUNKS, 2)),
-        dma((CHUNKS, 4)),
-        dma((CHUNKS, 4)),
+        dma((CHUNKS,)),
+        dma((CHUNKS,)),
         dma((samp_count,)),
         dma((samp_count,)),
         dma((2, samp_count, CHUNKS)),

time: 63 us -> 61.4 us (0.975)
  Pallas kernels: 61.3 us -> 59.7 us
    pallas_call x1, Pallas kernels: 61.3 us -> 59.7 us  [body(): pl.pallas_call(functools.partial(kernel, var_count, samp_count), out_shap...]
where the time goes in v6:
time: 61.4 us; the launch traced here: 61.2 us
  Pallas kernels  59.7 us (97%)
  local copies, waits for them, and re-layouts  1.56 us (3%)
    pallas_call x1, Pallas kernels, body(): pl.pallas_call(functools.partial(kernel, var_count, samp_count), out_shap...  59.7 us
    unnamed x3, local copies, waits for them, and re-layouts  1.56 us

profile of v6, /device:TPU:0, one launch (start us, length us, event | category | flops | bytes accessed | tf_op | source)
XLA Modules:
  0.0 61.2 jit_solution(7336284267594826351)
XLA Ops:
  0.0 0.0 copy-start
  0.0 0.7 %copy-done = s32[8,3]{0,1:T(4,128)S(1)} copy-done((s32[8,3]{0,1:T(4,128)S(1)}, s32[8,3]{0,1:T(4,128)}, u32[]{:S(2)}) %copy-start) | copy-done | bytes 120
  0.7 59.7 %shard_map.37 = f32[4,3,128,128]{3,2,1,0:T(8,128)S(1)} custom-call(bf16[512,1024]{1,0:T(8,128)(2,1)} %obs_ref.1, s32[3,8]{1,0:T(4,128)S(1)} %bitcast.1, bf16[8,3,128,128]{3,2,1,0:T(8,128)(2,1)} %omega_ref.1), custom_call_target="tpu_custom_call" | custom-call | tf_op jit(solution)/shard_map/pallas_call | solution.py:404
  60.4 0.9 %copy.5 = f32[4,3,128,128]{3,2,1,0:T(8,128)} copy(f32[4,3,128,128]{3,2,1,0:T(8,128)S(1)} %shard_map.37) | data formatting | bytes 1572864
Async XLA Ops:
  0.0 0.7 %copy-start = (s32[8,3]{0,1:T(4,128)S(1)}, s32[8,3]{0,1:T(4,128)}, u32[]{:S(2)}) copy-start(s32[8,3]{0,1:T(4,128)} %param.4) | copy-start | bytes 292

commit v7 on v6

--- a/solution.py
+++ b/solution.py
@@ -14,7 +14,7 @@
 THRESHOLD = 0.25
 EPSILON = 1e-06
 CHUNKS = 8
-AHEAD = 4
+AHEAD = 2
 
 
 def kernel(
@@ -136,6 +136,8 @@
     for copy in loads:
         copy.wait()
     pl.semaphore_wait(barrier, group - 1 + layers - 1)
+    load_table.wait()
+    table_copy = remote(table.at[0], table.at[1], table_send.at[0], table_recv.at[0], device(across, s))
     x_copies = []
     z_copies = []
     mate_copies = []
@@ -156,8 +158,6 @@
 
     for c in range(AHEAD):
         begin(c)
-    load_table.wait()
-    table_copy = remote(table.at[0], table.at[1], table_send.at[0], table_recv.at[0], device(across, s))
     own_copies = []
     for d in range(1, samp_count):
         peer = lax.rem(s + d, samp_count)
@@ -171,8 +171,8 @@
         z_copies[c].append(
             remote(strip(c, across_slot), strip(c, core * 4 + 3 * x), z_send.at[c, 1], z_recv.at[c, 1], device(target, s))
         )
-        if c + AHEAD < CHUNKS:
-            begin(c + AHEAD)
+        for later in range(AHEAD * (c + 1), min(AHEAD * (c + 2), CHUNKS)):
+            begin(later)
 
     def share_layers(c):
         for copy in z_copies[c]:
@@ -252,20 +252,20 @@
             else:
                 gram[r] += product
 
+    table_copy.wait_recv()
+    fetch = pltpu.make_async_copy(table, routes, load_sem.at[row_blocks + 2])
+    fetch.start()
+    fetch.wait()
+    for e in range(2):
+        for d in range(samp_count):
+            for k in range(1, slot_count):
+                for r in range(share):
+                    slots[e, d, k, r] = block_of(e, lax.rem(s + d, samp_count) * share + r, k)
+    load_omega.wait()
+
     for turn in range(CHUNKS + 5):
         if turn < CHUNKS:
             pass_on(turn)
-        if turn == 1:
-            table_copy.wait_recv()
-            fetch = pltpu.make_async_copy(table, routes, load_sem.at[row_blocks + 2])
-            fetch.start()
-            fetch.wait()
-            for e in range(2):
-                for d in range(samp_count):
-                    for k in range(1, slot_count):
-                        for r in range(share):
-                            slots[e, d, k, r] = block_of(e, lax.rem(s + d, samp_count) * share + r, k)
-            load_omega.wait()
         if 0 <= turn - 2 < CHUNKS:
             share_layers(turn - 2)
         if 0 <= turn - 3 < CHUNKS:

time: 61.4 us -> 63.1 us (1.028)
  Pallas kernels: 59.7 us -> 61.4 us
    pallas_call x1, Pallas kernels: 59.7 us -> 61.4 us  [body(): pl.pallas_call(functools.partial(kernel, var_count, samp_count), out_shap...]
where the time goes in v7:
time: 63.1 us; the launch traced here: 63 us
  Pallas kernels  61.4 us (97%)
  local copies, waits for them, and re-layouts  1.56 us (2%)
    pallas_call x1, Pallas kernels, body(): pl.pallas_call(functools.partial(kernel, var_count, samp_count), out_shap...  61.4 us
    unnamed x3, local copies, waits for them, and re-layouts  1.56 us

profile of v7, /device:TPU:0, one launch (start us, length us, event | category | flops | bytes accessed | tf_op | source)
XLA Modules:
  0.0 63.0 jit_solution(8133544174605709590)
XLA Ops:
  0.0 0.0 copy-start
  0.0 0.7 %copy-done = s32[8,3]{0,1:T(4,128)S(1)} copy-done((s32[8,3]{0,1:T(4,128)S(1)}, s32[8,3]{0,1:T(4,128)}, u32[]{:S(2)}) %copy-start) | copy-done | bytes 120
  0.7 61.4 %shard_map.37 = f32[4,3,128,128]{3,2,1,0:T(8,128)S(1)} custom-call(bf16[512,1024]{1,0:T(8,128)(2,1)} %obs_ref.1, s32[3,8]{1,0:T(4,128)S(1)} %bitcast.1, bf16[8,3,128,128]{3,2,1,0:T(8,128)(2,1)} %omega_ref.1), custom_call_target="tpu_custom_call" | custom-call | tf_op jit(solution)/shard_map/pallas_call | solution.py:404
  62.1 0.9 %copy.5 = f32[4,3,128,128]{3,2,1,0:T(8,128)} copy(f32[4,3,128,128]{3,2,1,0:T(8,128)S(1)} %shard_map.37) | data formatting | bytes 1572864
Async XLA Ops:
  0.0 0.7 %copy-start = (s32[8,3]{0,1:T(4,128)S(1)}, s32[8,3]{0,1:T(4,128)}, u32[]{:S(2)}) copy-start(s32[8,3]{0,1:T(4,128)} %param.4) | copy-start | bytes 292

commit v8 on v7

--- a/solution.py
+++ b/solution.py
@@ -14,7 +14,7 @@
 THRESHOLD = 0.25
 EPSILON = 1e-06
 CHUNKS = 8
-AHEAD = 2
+AHEAD = 8
 
 
 def kernel(

time: 63.1 us -> 65.9 us (1.044)
  Pallas kernels: 61.4 us -> 64.2 us
    pallas_call x1, Pallas kernels: 61.4 us -> 64.2 us  [body(): pl.pallas_call(functools.partial(kernel, var_count, samp_count), out_shap...]
where the time goes in v8:
time: 65.9 us; the launch traced here: 65.8 us
  Pallas kernels  64.2 us (97%)
  local copies, waits for them, and re-layouts  1.56 us (2%)
    pallas_call x1, Pallas kernels, body(): pl.pallas_call(functools.partial(kernel, var_count, samp_count), out_shap...  64.2 us
    unnamed x3, local copies, waits for them, and re-layouts  1.56 us

profile of v8, /device:TPU:0, one launch (start us, length us, event | category | flops | bytes accessed | tf_op | source)
XLA Modules:
  0.0 65.8 jit_solution(2430776445056891308)
XLA Ops:
  0.0 0.0 copy-start
  0.0 0.7 %copy-done = s32[8,3]{0,1:T(4,128)S(1)} copy-done((s32[8,3]{0,1:T(4,128)S(1)}, s32[8,3]{0,1:T(4,128)}, u32[]{:S(2)}) %copy-start) | copy-done | bytes 120
  0.7 64.2 %shard_map.37 = f32[4,3,128,128]{3,2,1,0:T(8,128)S(1)} custom-call(bf16[512,1024]{1,0:T(8,128)(2,1)} %obs_ref.1, s32[3,8]{1,0:T(4,128)S(1)} %bitcast.1, bf16[8,3,128,128]{3,2,1,0:T(8,128)(2,1)} %omega_ref.1), custom_call_target="tpu_custom_call" | custom-call | tf_op jit(solution)/shard_map/pallas_call | solution.py:404
  64.9 0.9 %copy.5 = f32[4,3,128,128]{3,2,1,0:T(8,128)} copy(f32[4,3,128,128]{3,2,1,0:T(8,128)S(1)} %shard_map.37) | data formatting | bytes 1572864
Async XLA Ops:
  0.0 0.7 %copy-start = (s32[8,3]{0,1:T(4,128)S(1)}, s32[8,3]{0,1:T(4,128)}, u32[]{:S(2)}) copy-start(s32[8,3]{0,1:T(4,128)} %param.4) | copy-start | bytes 292
